TPU v7x, 128 devices: a whole 4x4x4 slice. The times are simulated.
128 devices in a mesh: rep: 8 (over x_hi, y), fsdp: 16 (over z, x_lo, core).
Axes of the slice: x: 4 (x_hi: 2, x_lo: 2; x = x_hi * 2 + x_lo), y: 4, z: 4, core: 2. Of those that a mesh axis runs over, the one named last changes fastest.
Arguments:
- inner_weights: bfloat16 [8, 8192, 1024], P('rep', 'fsdp'), may hold values from -6 to 6
- master_weights: float32 [8, 8192, 1024], P('rep', 'fsdp'), may hold values from -6 to 6
- momentum: float32 [8, 8192, 1024], P('rep', 'fsdp'), may hold values from -6 to 6
- tokens: bfloat16 [8, 8192, 8192], P('rep', 'fsdp'), may hold values from -0.06591797 to 0.06591797
- partner: int32 [16, 8], P('fsdp'), may hold values from 0 to 7, as said below
Outputs:
- new_master: float32 [8, 8192, 1024], P('rep', 'fsdp')
- new_momentum: float32 [8, 8192, 1024], P('rep', 'fsdp')
- keys: bfloat16 [8, 8192, 1024], P('rep', 'fsdp')
Inputs may be any that keep to these rules, and one draw needn't show every extreme that they name: For each block s, partner[s, r] = r XOR m_s for one mask m_s with 1 <= m_s < 8, the same m_s for all r, so each row of partner is an involution without fixed points.
All inputs are finite; a program needn't handle non-finite values.
Results may differ from a plain program's by a relative error of at most 0.005.
Values may be sent and summed in bfloat16 or wider, within the bound.
A program may use at most 128 MiB of HBM per device.

v0:
```python
import jax
import jax.numpy as jnp
from jax import lax
from jax.sharding import PartitionSpec as P


def partner_2(value, axis, bit):
    return lax.ppermute(value, axis, [(i, i ^ 1 << bit) for i in range(lax.axis_size(axis))])


def cross_difference(payload, bit_index):
    return partner_2(payload, "rep", bit_index)


def reach_partner(payload, offset_mask, mover):
    level_count = lax.axis_size("rep").bit_length() - 1
    for bit_index in range(level_count):
        bit_set = jnp.bitwise_and(jnp.right_shift(offset_mask, bit_index), 1) == 1
        arrived = mover(payload, bit_index)
        payload = jax.tree.map(
            lambda new_part, old_part: jnp.where(bit_set, new_part, old_part), arrived, payload
        )
    return payload


def local(inner_weights, master_weights, momentum, tokens, partner):
    inner_local = inner_weights[0]
    master_local = master_weights[0]
    momentum_local = momentum[0]
    token_rows = tokens[0]
    here_index = lax.axis_index("rep")
    offset_mask = jnp.bitwise_xor(partner[0, here_index], here_index)
    difference = master_local - inner_local.astype(jnp.float32)
    mate_master, mate_difference = reach_partner(
        (master_local, difference), offset_mask, cross_difference
    )
    mean_difference = (difference + mate_difference) * 0.5
    mean_master = (master_local + mate_master) * 0.5
    new_momentum = 0.9 * momentum_local + mean_difference
    new_master = mean_master - 0.7 * (mean_difference + 0.9 * new_momentum)
    fresh = new_master.astype(jnp.bfloat16)
    key_sums = jnp.dot(
        token_rows,
        lax.all_gather(fresh, "fsdp", axis=0, tiled=True),
        preferred_element_type=jnp.float32,
    )
    return (new_master[None], new_momentum[None], key_sums.astype(jnp.bfloat16)[None])


def solution(mesh):
    return jax.shard_map(
        local,
        mesh=mesh,
        in_specs=(
            P("rep", "fsdp", None),
            P("rep", "fsdp", None),
            P("rep", "fsdp", None),
            P("rep", "fsdp", None),
            P("fsdp", None),
        ),
        out_specs=(P("rep", "fsdp", None), P("rep", "fsdp", None), P("rep", "fsdp", None)),
        check_vma=False,
    )
```

profile of v0, /device:TPU:1, one launch (start us, length us, event | category | flops | bytes accessed | tf_op | source)
XLA Modules:
  0.0 373.3 jit_solution(3927729829613198609)
XLA Ops:
  7.2 0.0 copy-start
  7.2 0.0 all-gather.2.cloned.1.call-start
  7.2 2.2 collective-permute-start
  9.4 0.0 copy-done
  9.4 0.6 constant_dynamic-slice_fusion
  10.7 44.0 %collective-permute-done = f32[512,1024]{1,0:T(8,128)} collective-permute-done((f32[512,1024]{1,0:T(8,128)}, f32[512,1024]{1,0:T(8,128)}, u32[]{:S(2)}, u32[]{:S(2)}) %collective-permute-start) | collective-permute-done | bytes 2097184 | tf_op jit(solution)/shard_map/ppermute | solution.py:8
  54.7 4.6 %broadcast_select_fusion.1 = (f32[512,1024]{1,0:T(8,128)}, f32[512,1024]{1,0:T(8,128)S(1)}) fusion(f32[512,1024]{1,0:T(8,128)} %collective-permute-done, pred[]{:T(512)S(6)} %eq.11, f32[1,512,1024]{2,1,0:T(8,128)} %param.6, bf16[1,512,1024]{2,1,0:T(8,128)(2,1)} %param.5), kind=kLoop, calls=%fused_computation.10 | loop fusion | flops 1572864 | bytes 9437185 | tf_op jit(solution)/shard_map/jit(_where)/select_n | solution.py:21
  59.3 1.6 collective-permute-start.3
  60.8 2.6 collective-permute-start.1
  63.5 42.1 %collective-permute-done.3 = f32[512,1024]{1,0:T(8,128)S(1)} collective-permute-done((f32[512,1024]{1,0:T(8,128)S(1)}, f32[512,1024]{1,0:T(8,128)S(1)}, u32[]{:S(2)}, u32[]{:S(2)}) %collective-permute-start.3) | collective-permute-done | bytes 2097184 | tf_op jit(solution)/shard_map/ppermute | solution.py:8
  105.6 1.7 broadcast_select_fusion
  107.3 3.1 collective-permute-start.4
  110.4 42.9 %collective-permute-done.1 = f32[512,1024]{1,0:T(8,128)} collective-permute-done((f32[512,1024]{1,0:T(8,128)}, f32[512,1024]{1,0:T(8,128)}, u32[]{:S(2)}, u32[]{:S(2)}) %collective-permute-start.1) | collective-permute-done | bytes 2097184 | tf_op jit(solution)/shard_map/ppermute | solution.py:8
  153.3 3.5 broadcast_select_fusion.3
  156.7 2.7 collective-permute-start.2
  159.5 38.7 %collective-permute-done.4 = f32[512,1024]{1,0:T(8,128)} collective-permute-done((f32[512,1024]{1,0:T(8,128)}, f32[512,1024]{1,0:T(8,128)}, u32[]{:S(2)}, u32[]{:S(2)}) %collective-permute-start.4) | collective-permute-done | bytes 2097184 | tf_op jit(solution)/shard_map/ppermute | solution.py:8
  198.2 3.5 broadcast_select_fusion.2
  201.7 2.7 collective-permute-start.5
  204.4 0.0 collective-permute-done.2
  204.4 44.4 %collective-permute-done.5 = f32[512,1024]{1,0:T(8,128)} collective-permute-done((f32[512,1024]{1,0:T(8,128)}, f32[512,1024]{1,0:T(8,128)}, u32[]{:S(2)}, u32[]{:S(2)}) %collective-permute-start.5) | collective-permute-done | bytes 2097184 | tf_op jit(solution)/shard_map/ppermute | solution.py:8
  248.8 7.9 %fusion.9 = (bf16[512,1024]{1,0:T(8,128)(2,1)}, f32[512,1024]{1,0:T(8,128)}, f32[1,512,1024]{2,1,0:T(8,128)}) fusion(f32[1,512,1024]{2,1,0:T(8,128)} %param.7, f32[512,1024]{1,0:T(8,128)S(1)} %get-tuple-element.10, f32[512,1024]{1,0:T(8,128)} %collective-permute-done.5, f32[512,1024]{1,0:T(8,128)} %broadcast_select_fusion.2, ...), kind=kLoop, calls=%fused_computation.14 | loop fusion | flops 6815744 | bytes 19922944 | tf_op jit(solution)/shard_map/convert_element_type | solution.py:41
  256.7 0.0 all-gather.2.cloned.1.call-update
  256.7 93.5 %all-gather.2.cloned.1.call-done = bf16[8192,1024]{1,0:T(8,128)(2,1)} async-done(((bf16[512,1024]{1,0:T(8,128)(2,1)}), bf16[8192,1024]{1,0:T(8,128)(2,1)}) %all-gather.2.cloned.1.call-update) | async-done | bytes 16777232 | tf_op jit(solution)/shard_map/all_gather | solution.py:44
  350.2 14.9 %fusion.6 = bf16[1,512,1024]{1,2,0:T(8,128)(2,1)S(1)} fusion(bf16[8192,1024]{1,0:T(8,128)(2,1)} %all-gather.2.cloned.1.call-done, bf16[1,512,8192]{2,1,0:T(8,128)(2,1)} %param.8), kind=kOutput, calls=%fused_computation.8 | convolution fusion | flops 8590458880 | bytes 26214400 | tf_op jit(solution)/shard_map/dot_general | solution.py:42
  365.1 1.3 copy.8
Async XLA Ops:
  7.2 2.3 copy-start
  7.2 343.0 %all-gather.2.cloned.1.call-start = ((), (), s32[]{:S(2)}) async-start(), calls=%async_computation | async-start | bytes 17825792 | tf_op jit(solution)/shard_map/all_gather | solution.py:44
  7.2 47.5 %collective-permute-start = (f32[512,1024]{1,0:T(8,128)}, f32[512,1024]{1,0:T(8,128)}, u32[]{:S(2)}, u32[]{:S(2)}) collective-permute-start(f32[512,1024]{1,0:T(8,128)} %bitcast.31), channel_id=1, source_target_pairs={{0,16},{16,0},{32,48},{48,32},{64,80},{80,64},{96,112},{112,96},{1... | collective-permute-start | bytes 6291464 | tf_op jit(solution)/shard_map/ppermute | solution.py:8
  59.3 46.3 %collective-permute-start.3 = (f32[512,1024]{1,0:T(8,128)S(1)}, f32[512,1024]{1,0:T(8,128)S(1)}, u32[]{:S(2)}, u32[]{:S(2)}) collective-permute-start(f32[512,1024]{1,0:T(8,128)S(1)} %get-tuple-element.10), channel_id=1, source_target_pairs={{0,16},{16,0},{32,48},{48,32},{64,80},{80,64},{96,112},{112,96},{1... | collective-permute-start | bytes 6291464 | tf_op jit(solution)/shard_map/ppermute | solution.py:8
  60.8 92.4 %collective-permute-start.1 = (f32[512,1024]{1,0:T(8,128)}, f32[512,1024]{1,0:T(8,128)}, u32[]{:S(2)}, u32[]{:S(2)}) collective-permute-start(f32[512,1024]{1,0:T(8,128)} %get-tuple-element.9), channel_id=1, source_target_pairs={{0,32},{16,48},{32,0},{48,16},{64,96},{80,112},{96,64},{112,80},{1... | collective-permute-start | bytes 6291464 | tf_op jit(solution)/shard_map/ppermute | solution.py:8
  107.3 90.9 %collective-permute-start.4 = (f32[512,1024]{1,0:T(8,128)}, f32[512,1024]{1,0:T(8,128)}, u32[]{:S(2)}, u32[]{:S(2)}) collective-permute-start(f32[512,1024]{1,0:T(8,128)} %broadcast_select_fusion), channel_id=1, source_target_pairs={{0,32},{16,48},{32,0},{48,16},{64,96},{80,112},{96,64},{112,80},{1... | collective-permute-start | bytes 6291464 | tf_op jit(solution)/shard_map/ppermute | solution.py:8
  156.7 47.7 %collective-permute-start.2 = (f32[512,1024]{1,0:T(8,128)}, f32[512,1024]{1,0:T(8,128)}, u32[]{:S(2)}, u32[]{:S(2)}) collective-permute-start(f32[512,1024]{1,0:T(8,128)} %broadcast_select_fusion.3), channel_id=1, source_target_pairs={{0,64},{16,80},{32,96},{48,112},{64,0},{80,16},{96,32},{112,48},{1... | collective-permute-start | bytes 6291464 | tf_op jit(solution)/shard_map/ppermute | solution.py:8
  201.7 47.1 %collective-permute-start.5 = (f32[512,1024]{1,0:T(8,128)}, f32[512,1024]{1,0:T(8,128)}, u32[]{:S(2)}, u32[]{:S(2)}) collective-permute-start(f32[512,1024]{1,0:T(8,128)} %broadcast_select_fusion.2), channel_id=1, source_target_pairs={{0,64},{16,80},{32,96},{48,112},{64,0},{80,16},{96,32},{112,48},{1... | collective-permute-start | bytes 6291464 | tf_op jit(solution)/shard_map/ppermute | solution.py:8
Sparse Core Ops, SparseCore 0:
  256.9 93.3 all-gather.1
where the time goes:
time: 374 us; the launch traced here: 373 us
  waiting for transfers between devices  306 us (82%)
  other arithmetic  21.2 us (6%)
  starting transfers between devices  15 us (4%)
  matrix products  14.9 us (4%)
  between operations  14.7 us (4%)
    ppermute x6, waiting for transfers between devices, partner_2(): lax.ppermute(value, axis, [(i, i ^ 1 << bit) for i in range(lax.axis_size...  212 us
    all_gather x1, waiting for transfers between devices, local(): lax.all_gather(fresh, 'fsdp', axis=0, tiled=True)  93.5 us
    ppermute x6, starting transfers between devices, partner_2(): lax.ppermute(value, axis, [(i, i ^ 1 << bit) for i in range(lax.axis_size...  14.9 us
    dot_general x1, matrix products, local(): jnp.dot(token_rows, lax.all_gather(fresh, 'fsdp', axis=0, tiled=True), pr...  14.9 us
    select_n x4, other arithmetic, reach_partner(): jnp.where(bit_set, new_part, old_part)  13.3 us
    convert_element_type x1, other arithmetic, local(): fresh = new_master.astype(jnp.bfloat16)  7.91 us
  transfers between devices with their start and end apart: 7, of which 6 were waited for; matrix products, arithmetic and copies ran while one was open for 2% of the time, Pallas kernels for 0%

commit v1 on v0

v1 whole, which is shorter than its diff:
```python
import functools

import jax
import jax.numpy as jnp
from jax import lax
from jax.experimental import pallas as pl
from jax.experimental.pallas import tpu as pltpu
from jax.sharding import PartitionSpec as P

MESH = pl.DeviceIdType.MESH
R, W = 64, 256
OFF_B, OFF_X, OFF_U, OFF_Z, OFF_F, OFF_D, OFF_M = 1, 2, 3, 4, 5, 6, 7


def kernel(
    part_ref, inner_ref, master_ref, mom_ref, tok_ref,
    out_master, out_mom, out_keys,
    m_v, mom_v, pay, buf_a, buf_b, buf_x, nm_v, nmom_v, fresh, tok_v, keys_v, acc,
    load_sem, send_sem, ra, rb, rx, rs, rz, rf, rd, out_sem,
):
    J = master_ref.shape[0]
    G = master_ref.shape[2] // W
    C = G * J
    slots_per_tick = 16 // J
    rows = J * R

    rep = lax.axis_index("rep")
    fs = lax.axis_index("fsdp")
    rep1 = rep + 1 - 2 * lax.rem(rep, 2)
    rep3 = rep + 3 - 2 * lax.rem(rep, 4)
    rep4 = lax.rem(rep + 4, 8)
    core = lax.rem(fs, 2)
    xlo = lax.rem(lax.div(fs, 2), 2)
    z = lax.div(fs, 4)
    sib = fs + 1 - 2 * core
    xn = fs + 2 - 4 * xlo
    zu = lax.rem(fs + 4, 16)
    zd = lax.rem(fs + 12, 16)

    dev_a, dev_b, dev_x = (rep1, fs), (rep3, fs), (rep4, fs)
    dev_s, dev_u, dev_d, dev_c = (rep, xn), (rep, zu), (rep, zd), (rep, sib)

    def load_mi(g):
        cols = pl.ds(g * W, W)
        return (
            pltpu.make_async_copy(master_ref.at[:, :, cols], m_v.at[pl.ds(g * J, J)], load_sem.at[0, g]),
            pltpu.make_async_copy(inner_ref.at[:, :, cols], pay.at[pl.ds(g * J, J), 1], load_sem.at[1, g]),
        )

    def load_mom(g):
        return pltpu.make_async_copy(mom_ref.at[:, :, pl.ds(g * W, W)], mom_v.at[pl.ds(g * J, J)], load_sem.at[2, g])

    load_tok = pltpu.make_async_copy(tok_ref, tok_v, load_sem.at[3, 0])
    for g in range(G):
        for c in load_mi(g):
            c.start()
    for g in range(G):
        load_mom(g).start()
    load_tok.start()

    barrier = pltpu.get_barrier_semaphore()
    for d in (dev_a, dev_b, dev_x, dev_s, dev_u, dev_d, dev_c):
        pl.semaphore_signal(barrier, inc=1, device_id=d, device_id_type=MESH)
    pl.semaphore_wait(barrier, 7)
    for g in range(G):
        for c in load_mi(g):
            c.wait()

    mask = jnp.bitwise_xor(part_ref[0, rep], rep)
    bit1 = lax.rem(lax.div(mask, 2), 2)
    pick_a = lax.rem(lax.rem(mask, 2) + bit1, 2) == 1
    pick_b = bit1 == 1
    pick_x = lax.div(mask, 4) == 1

    def remote(src, dst, k, recv, dev):
        return pltpu.make_async_remote_copy(
            src_ref=src, dst_ref=dst, send_sem=send_sem.at[k], recv_sem=recv, device_id=dev, device_id_type=MESH
        )

    def copy_a(t):
        return remote(pay.at[t], buf_a.at[t], 0, ra.at[t], dev_a)

    def copy_b(t):
        return remote(buf_a.at[t], buf_b.at[t], 1, rb.at[t], dev_b)

    def copy_x(t):
        return remote(buf_b.at[t], buf_x.at[t], 2, rx.at[t], dev_x)

    def copy_s(t):
        return remote(fresh.at[t, 0], fresh.at[t, 1], 3, rs.at[t], dev_s)

    def copy_up(t):
        return remote(fresh.at[t, pl.ds(0, 2)], fresh.at[t, pl.ds(6, 2)], 4, rz.at[0, t], dev_u)

    def copy_down(t):
        return remote(fresh.at[t, pl.ds(0, 2)], fresh.at[t, pl.ds(2, 2)], 5, rz.at[1, t], dev_d)

    def copy_fup(t):
        return remote(fresh.at[t, 6], fresh.at[t, 4], 6, rf.at[0, t], dev_u)

    def copy_fdown(t):
        return remote(fresh.at[t, 3], fresh.at[t, 5], 7, rf.at[1, t], dev_d)

    def copy_c(t):
        return remote(fresh.at[t, pl.ds(0, 8)], fresh.at[t, pl.ds(8, 8)], 8, rd.at[t], dev_c)

    def out_copies(g):
        cols = pl.ds(pl.multiple_of(g * W, W), W)
        span = pl.ds(g * J, J)
        return (
            pltpu.make_async_copy(nm_v.at[span], out_master.at[:, :, cols], out_sem.at[0, g]),
            pltpu.make_async_copy(nmom_v.at[span], out_mom.at[:, :, cols], out_sem.at[1, g]),
        )

    def out_key(g):
        cols = pl.ds(pl.multiple_of(g * W, W), W)
        return pltpu.make_async_copy(keys_v.at[g], out_keys.at[:, cols], out_sem.at[2, g])

    def tick(t, _):
        @pl.when(t < C)
        def _():
            pay[t, 0] = m_v[t].astype(jnp.bfloat16)
            copy_a(t).start()

        tb = t - OFF_B

        @pl.when((tb >= 0) & (tb < C))
        def _():
            copy_a(tb).wait_recv()
            buf_a[tb] = jnp.where(pick_a, buf_a[tb], pay[tb])
            copy_b(tb).start()

        tx = t - OFF_X

        @pl.when((tx >= 0) & (tx < C))
        def _():
            copy_b(tx).wait_recv()
            buf_b[tx] = jnp.where(pick_b, buf_b[tx], buf_a[tx])
            copy_x(tx).start()

        tu = t - OFF_U

        @pl.when(tu == 0)
        def _():
            for g in range(G):
                load_mom(g).wait()

        @pl.when((tu >= 0) & (tu < C))
        def _():
            copy_x(tu).wait_recv()
            their = jnp.where(pick_x, buf_x[tu], buf_b[tu])
            their_m = their[0].astype(jnp.float32)
            their_i = their[1].astype(jnp.float32)
            own_m = m_v[tu]
            own_i = pay[tu, 1].astype(jnp.float32)
            mean_d = ((own_m - own_i) + (their_m - their_i)) * 0.5
            mean_m = (own_m + their_m) * 0.5
            new_mom = 0.9 * mom_v[tu] + mean_d
            new_m = mean_m - 0.7 * (mean_d + 0.9 * new_mom)
            nmom_v[tu] = new_mom
            nm_v[tu] = new_m
            fresh[tu, 0] = new_m.astype(jnp.bfloat16)
            copy_s(tu).start()

        @pl.when((tu >= 0) & (tu < C) & (lax.rem(tu + C, J) == J - 1))
        def _():
            for c in out_copies(lax.div(tu, J)):
                c.start()

        tz = t - OFF_Z

        @pl.when((tz >= 0) & (tz < C))
        def _():
            copy_s(tz).wait_recv()
            copy_up(tz).start()
            copy_down(tz).start()

        tf = t - OFF_F

        @pl.when((tf >= 0) & (tf < C))
        def _():
            copy_up(tf).wait_recv()
            copy_fup(tf).start()
            copy_down(tf).wait_recv()
            copy_fdown(tf).start()

        td = t - OFF_D

        @pl.when((td >= 0) & (td < C))
        def _():
            copy_fup(td).wait_recv()
            copy_fdown(td).wait_recv()
            copy_c(td).start()

        tm = t - OFF_M

        @pl.when((tm >= 0) & (tm < C))
        def _():
            copy_c(tm).wait_recv()

        @pl.when(tm == J - 1)
        def _():
            load_tok.wait()

        u = tm - (J - 1)

        @pl.when(u >= 0)
        def _():
            g = lax.div(u, J)
            k = lax.rem(u, J)
            total = jnp.where(k == 0, 0.0, acc[...])
            for i in range(slots_per_tick):
                slot = k * slots_per_tick + i
                half = lax.div(slot, 8)
                low = lax.rem(slot, 8)
                oz = lax.rem(z + lax.div(low, 2), 4)
                ox = lax.rem(xlo + low, 2)
                oc = lax.rem(core + half, 2)
                owner = oz * 4 + ox * 2 + oc
                cols = pl.ds(pl.multiple_of(owner * rows, rows), rows)
                rhs = fresh[pl.ds(g * J, J), slot].reshape(rows, W)
                total += jnp.dot(tok_v[:, cols], rhs, preferred_element_type=jnp.float32)
            acc[...] = total

            @pl.when(k == J - 1)
            def _():
                keys_v[g] = total.astype(jnp.bfloat16)
                out_key(g).start()

        return 0

    lax.fori_loop(0, OFF_M + C + J - 1, tick, 0)

    everything = (
        (pay, buf_a, 0, ra.at[0], dev_a),
        (buf_a, buf_b, 1, rb.at[0], dev_b),
        (buf_b, buf_x, 2, rx.at[0], dev_x),
        (fresh.at[:, 0], fresh.at[:, 1], 3, rs.at[0], dev_s),
        (fresh.at[:, pl.ds(0, 2)], fresh.at[:, pl.ds(6, 2)], 4, rz.at[0, 0], dev_u),
        (fresh.at[:, pl.ds(0, 2)], fresh.at[:, pl.ds(2, 2)], 5, rz.at[1, 0], dev_d),
        (fresh.at[:, 6], fresh.at[:, 4], 6, rf.at[0, 0], dev_u),
        (fresh.at[:, 3], fresh.at[:, 5], 7, rf.at[1, 0], dev_d),
        (fresh.at[:, pl.ds(0, 8)], fresh.at[:, pl.ds(8, 8)], 8, rd.at[0], dev_c),
    )
    for src, dst, k, recv, dev in everything:
        remote(src, dst, k, recv, dev).wait_send()
    for g in range(G):
        for c in out_copies(g):
            c.wait()
        out_key(g).wait()


def local(inner_weights, master_weights, momentum, tokens, partner):
    rows, cols = master_weights.shape[1:]
    toks, depth = tokens.shape[1:]
    J, G = rows // R, cols // W
    C = G * J
    bf16, f32 = jnp.bfloat16, jnp.float32
    anyspace = pl.BlockSpec(memory_space=pl.ANY)
    dma = pltpu.SemaphoreType.DMA
    new_master, new_mom, keys = pl.pallas_call(
        kernel,
        out_shape=(
            jax.ShapeDtypeStruct((J, R, cols), f32),
            jax.ShapeDtypeStruct((J, R, cols), f32),
            jax.ShapeDtypeStruct((toks, cols), bf16),
        ),
        in_specs=[pl.BlockSpec(memory_space=pltpu.SMEM)] + [anyspace] * 4,
        out_specs=(anyspace,) * 3,
        scratch_shapes=[
            pltpu.VMEM((C, R, W), f32),
            pltpu.VMEM((C, R, W), f32),
            pltpu.VMEM((C, 2, R, W), bf16),
            pltpu.VMEM((C, 2, R, W), bf16),
            pltpu.VMEM((C, 2, R, W), bf16),
            pltpu.VMEM((C, 2, R, W), bf16),
            pltpu.VMEM((C, R, W), f32),
            pltpu.VMEM((C, R, W), f32),
            pltpu.VMEM((C, 16, R, W), bf16),
            pltpu.VMEM((toks, depth), bf16),
            pltpu.VMEM((G, toks, W), bf16),
            pltpu.VMEM((toks, W), f32),
            dma((4, G)),
            dma((9,)),
            dma((C,)),
            dma((C,)),
            dma((C,)),
            dma((C,)),
            dma((2, C)),
            dma((2, C)),
            dma((C,)),
            dma((3, G)),
        ],
        compiler_params=pltpu.CompilerParams(
            collective_id=0, has_side_effects=True, vmem_limit_bytes=60 * 1024 * 1024
        ),
        cost_estimate=pl.CostEstimate(
            flops=2 * toks * depth * cols, bytes_accessed=18 * 1024 * 1024, transcendentals=0
        ),
        name="gossip_keys",
    )(
        partner,
        inner_weights.reshape(J, R, cols),
        master_weights.reshape(J, R, cols),
        momentum.reshape(J, R, cols),
        tokens[0],
    )
    return (
        new_master.reshape(1, rows, cols),
        new_mom.reshape(1, rows, cols),
        keys[None],
    )


def solution(mesh):
    return jax.shard_map(
        local,
        mesh=mesh,
        in_specs=(
            P("rep", "fsdp", None),
            P("rep", "fsdp", None),
            P("rep", "fsdp", None),
            P("rep", "fsdp", None),
            P("fsdp", None),
        ),
        out_specs=(P("rep", "fsdp", None), P("rep", "fsdp", None), P("rep", "fsdp", None)),
        check_vma=False,
    )
```

time: 374 us -> 152 us (0.41)
  waiting for transfers between devices: 306 us -> 0 us
  Pallas kernels: 0 us -> 145 us
  other arithmetic: 21.2 us -> 0 us
  starting transfers between devices: 15 us -> 0 us
  matrix products: 14.9 us -> 0 us
  between operations: 14.7 us -> 0.65 us
  local copies, waits for them, and re-layouts: 1.91 us -> 6.24 us
    ppermute x6 -> x0, waiting for transfers between devices: 212 us -> none  [partner_2(): lax.ppermute(value, axis, [(i, i ^ 1 << bit) for i in range(lax.axis_size...]
    pallas_call x0 -> x1, Pallas kernels: none -> 145 us  [local(): pl.pallas_call(kernel, out_shape=(jax.ShapeDtypeStruct((J, R, cols), f32)...]
    all_gather x1 -> x0, waiting for transfers between devices: 93.5 us -> none  [local(): lax.all_gather(fresh, 'fsdp', axis=0, tiled=True)]
    ppermute x6 -> x0, starting transfers between devices: 14.9 us -> none  [partner_2(): lax.ppermute(value, axis, [(i, i ^ 1 << bit) for i in range(lax.axis_size...]
    dot_general x1 -> x0, matrix products: 14.9 us -> none  [local(): jnp.dot(token_rows, lax.all_gather(fresh, 'fsdp', axis=0, tiled=True), pr...]
    select_n x4 -> x0, other arithmetic: 13.3 us -> none  [reach_partner(): jnp.where(bit_set, new_part, old_part)]
    convert_element_type x1 -> x0, other arithmetic: 7.91 us -> none  [local(): fresh = new_master.astype(jnp.bfloat16)]
    unnamed x3 -> x7, local copies, waits for them, and re-layouts: 1.32 us -> 6.24 us
  transfers between devices with their start and end apart: 7 -> 0, of which waited for: 6 -> 0; matrix products, arithmetic and copies ran while one was open for 2% -> 0% of each run, Pallas kernels for 0% -> 0%
where the time goes in v1:
time: 152 us; the launch traced here: 151 us
  Pallas kernels  145 us (95%)
  local copies, waits for them, and re-layouts  6.24 us (4%)
    pallas_call x1, Pallas kernels, local(): pl.pallas_call(kernel, out_shape=(jax.ShapeDtypeStruct((J, R, cols), f32)...  145 us
    unnamed x7, local copies, waits for them, and re-layouts  6.24 us

profile of v1, /device:TPU:1, one launch (start us, length us, event | category | flops | bytes accessed | tf_op | source)
XLA Modules:
  0.0 151.5 jit_solution(1051084120621645484)
XLA Ops:
  0.6 144.6 %gossip_keys.1 = (f32[8,64,1024]{2,1,0:T(8,128)}, f32[8,64,1024]{2,1,0:T(8,128)}, bf16[512,1024]{1,0:T(8,128)(2,1)}) custom-call(s32[1,8]{1,0:T(1,128)} %part_ref.1, bf16[8,64,1024]{2,1,0:T(8,128)(2,1)} %bitcast.13, f32[8,64,1024]{2,1,0:T(8,128)} %bitcast.11, f32[8,64,1024]{2,1,0:T(8,128)} %bitcast.12, bf16[512,8192]{1,0:T(8,128)(2,1)} %bitcast.10), custom_call_target="tpu_custom_call" | custom-call | flops 8589934592 | bytes 18874368 | tf_op jit(solution)/shard_map/gossip_keys/pallas_call | solution.py:261
  145.2 0.0 copy-start
  145.2 3.3 %copy.11 = f32[1,512,1024]{2,1,0:T(8,128)} copy(f32[1,512,1024]{2,1,0:T(8,128)} %bitcast.8) | data formatting | bytes 4194304
  148.5 0.0 copy-done
  148.5 0.0 copy-start.1
  148.5 1.3 copy.12
  149.8 0.6 copy-done.1
  150.5 1.0 copy.13
Async XLA Ops:
  145.2 3.3 %copy-start = (f32[8,64,1024]{2,1,0:T(8,128)S(1)}, f32[8,64,1024]{2,1,0:T(8,128)}, u32[]{:S(2)}) copy-start(f32[8,64,1024]{2,1,0:T(8,128)} %get-tuple-element.7) | copy-start | bytes 6291460
  148.5 2.0 %copy-start.1 = (bf16[512,1024]{1,0:T(8,128)(2,1)S(1)}, bf16[512,1024]{1,0:T(8,128)(2,1)}, u32[]{:S(2)}) copy-start(bf16[512,1024]{1,0:T(8,128)(2,1)} %get-tuple-element.8) | copy-start | bytes 3145732

commit v2 on v1

--- a/solution.py
+++ b/solution.py
@@ -9,7 +9,8 @@
 
 MESH = pl.DeviceIdType.MESH
 R, W = 64, 256
-OFF_B, OFF_X, OFF_U, OFF_Z, OFF_F, OFF_D, OFF_M = 1, 2, 3, 4, 5, 6, 7
+SUB = 128
+OFF_B, OFF_X, OFF_U, OFF_Z, OFF_F, OFF_D, OFF_M = 2, 4, 6, 8, 10, 12, 14
 
 
 def kernel(
@@ -21,7 +22,8 @@
     J = master_ref.shape[0]
     G = master_ref.shape[2] // W
     C = G * J
-    slots_per_tick = 16 // J
+    Q = SUB // R
+    slots_per_tick = 16 // Q
     rows = J * R
 
     rep = lax.axis_index("rep")
@@ -54,17 +56,14 @@
     for g in range(G):
         for c in load_mi(g):
             c.start()
-    for g in range(G):
-        load_mom(g).start()
-    load_tok.start()
 
     barrier = pltpu.get_barrier_semaphore()
     for d in (dev_a, dev_b, dev_x, dev_s, dev_u, dev_d, dev_c):
         pl.semaphore_signal(barrier, inc=1, device_id=d, device_id_type=MESH)
     pl.semaphore_wait(barrier, 7)
     for g in range(G):
-        for c in load_mi(g):
-            c.wait()
+        load_mom(g).start()
+    load_tok.start()
 
     mask = jnp.bitwise_xor(part_ref[0, rep], rep)
     bit1 = lax.rem(lax.div(mask, 2), 2)
@@ -88,6 +87,12 @@
 
     def copy_s(t):
         return remote(fresh.at[t, 0], fresh.at[t, 1], 3, rs.at[t], dev_s)
+
+    def copy_up_one(t, slot):
+        return remote(fresh.at[t, slot], fresh.at[t, 6 + slot], 4, rz.at[0, t], dev_u)
+
+    def copy_down_one(t, slot):
+        return remote(fresh.at[t, slot], fresh.at[t, 2 + slot], 5, rz.at[1, t], dev_d)
 
     def copy_up(t):
         return remote(fresh.at[t, pl.ds(0, 2)], fresh.at[t, pl.ds(6, 2)], 4, rz.at[0, t], dev_u)
@@ -117,6 +122,12 @@
         return pltpu.make_async_copy(keys_v.at[g], out_keys.at[:, cols], out_sem.at[2, g])
 
     def tick(t, _):
+        for g in range(G):
+            @pl.when(t == g * J)
+            def _():
+                for c in load_mi(g):
+                    c.wait()
+
         @pl.when(t < C)
         def _():
             pay[t, 0] = m_v[t].astype(jnp.bfloat16)
@@ -161,6 +172,8 @@
             nm_v[tu] = new_m
             fresh[tu, 0] = new_m.astype(jnp.bfloat16)
             copy_s(tu).start()
+            copy_up_one(tu, 0).start()
+            copy_down_one(tu, 0).start()
 
         @pl.when((tu >= 0) & (tu < C) & (lax.rem(tu + C, J) == J - 1))
         def _():
@@ -172,8 +185,8 @@
         @pl.when((tz >= 0) & (tz < C))
         def _():
             copy_s(tz).wait_recv()
-            copy_up(tz).start()
-            copy_down(tz).start()
+            copy_up_one(tz, 1).start()
+            copy_down_one(tz, 1).start()
 
         tf = t - OFF_F
 
@@ -198,17 +211,21 @@
         def _():
             copy_c(tm).wait_recv()
 
-        @pl.when(tm == J - 1)
+        @pl.when(tm == Q - 1)
         def _():
             load_tok.wait()
 
-        u = tm - (J - 1)
+        u = tm - (Q - 1)
 
         @pl.when(u >= 0)
         def _():
-            g = lax.div(u, J)
-            k = lax.rem(u, J)
-            total = jnp.where(k == 0, 0.0, acc[...])
+            q = lax.div(u, Q)
+            k = lax.rem(u, Q)
+            per_group = rows // SUB
+            g = lax.div(q, per_group)
+            part = lax.rem(q, per_group)
+            first = (part == 0) & (k == 0)
+            left, right = [], []
             for i in range(slots_per_tick):
                 slot = k * slots_per_tick + i
                 half = lax.div(slot, 8)
@@ -217,19 +234,28 @@
                 ox = lax.rem(xlo + low, 2)
                 oc = lax.rem(core + half, 2)
                 owner = oz * 4 + ox * 2 + oc
-                cols = pl.ds(pl.multiple_of(owner * rows, rows), rows)
-                rhs = fresh[pl.ds(g * J, J), slot].reshape(rows, W)
-                total += jnp.dot(tok_v[:, cols], rhs, preferred_element_type=jnp.float32)
-            acc[...] = total
-
-            @pl.when(k == J - 1)
+                left.append(tok_v[:, pl.ds(pl.multiple_of(owner * rows + part * SUB, SUB), SUB)])
+                right.append(fresh[pl.ds(q * Q, Q), slot].reshape(SUB, W))
+            product = jnp.dot(
+                jnp.concatenate(left, axis=1), jnp.concatenate(right, axis=0), preferred_element_type=jnp.float32
+            )
+
+            @pl.when(first)
             def _():
-                keys_v[g] = total.astype(jnp.bfloat16)
+                acc[...] = product
+
+            @pl.when(jnp.logical_not(first))
+            def _():
+                acc[...] += product
+
+            @pl.when((part == per_group - 1) & (k == Q - 1))
+            def _():
+                keys_v[g] = acc[...].astype(jnp.bfloat16)
                 out_key(g).start()
 
         return 0
 
-    lax.fori_loop(0, OFF_M + C + J - 1, tick, 0)
+    lax.fori_loop(0, OFF_M + C + Q - 1, tick, 0)
 
     everything = (
         (pay, buf_a, 0, ra.at[0], dev_a),

time: 152 us -> 109 us (0.72)
  Pallas kernels: 145 us -> 102 us
    pallas_call x1, Pallas kernels: 145 us -> 102 us  [local(): pl.pallas_call(kernel, out_shape=(jax.ShapeDtypeStruct((J, R, cols), f32)...]
where the time goes in v2:
time: 109 us
  Pallas kernels  102 us (94%)
  local copies, waits for them, and re-layouts  6.24 us (6%)
    pallas_call x1, Pallas kernels, local(): pl.pallas_call(kernel, out_shape=(jax.ShapeDtypeStruct((J, R, cols), f32)...  102 us
    unnamed x7, local copies, waits for them, and re-layouts  6.24 us

profile of v2, /device:TPU:1, one launch (start us, length us, event | category | flops | bytes accessed | tf_op | source)
XLA Modules:
  0.0 108.6 jit_solution(9666991996821991310)
XLA Ops:
  0.6 101.7 %gossip_keys.1 = (f32[8,64,1024]{2,1,0:T(8,128)}, f32[8,64,1024]{2,1,0:T(8,128)}, bf16[512,1024]{1,0:T(8,128)(2,1)}) custom-call(s32[1,8]{1,0:T(1,128)} %part_ref.1, bf16[8,64,1024]{2,1,0:T(8,128)(2,1)} %bitcast.13, f32[8,64,1024]{2,1,0:T(8,128)} %bitcast.11, f32[8,64,1024]{2,1,0:T(8,128)} %bitcast.12, bf16[512,8192]{1,0:T(8,128)(2,1)} %bitcast.10), custom_call_target="tpu_custom_call" | custom-call | flops 8589934592 | bytes 18874368 | tf_op jit(solution)/shard_map/gossip_keys/pallas_call | solution.py:287
  102.3 0.0 copy-start
  102.3 3.3 %copy.11 = f32[1,512,1024]{2,1,0:T(8,128)} copy(f32[1,512,1024]{2,1,0:T(8,128)} %bitcast.8) | data formatting | bytes 4194304
  105.7 0.0 copy-done
  105.7 0.0 copy-start.1
  105.7 1.3 %copy.12 = f32[1,512,1024]{2,1,0:T(8,128)} copy(f32[1,512,1024]{2,1,0:T(8,128)S(1)} %bitcast.7) | data formatting | bytes 4194304
  107.0 0.6 copy-done.1
  107.6 1.0 copy.13
Async XLA Ops:
  102.3 3.3 %copy-start = (f32[8,64,1024]{2,1,0:T(8,128)S(1)}, f32[8,64,1024]{2,1,0:T(8,128)}, u32[]{:S(2)}) copy-start(f32[8,64,1024]{2,1,0:T(8,128)} %get-tuple-element.7) | copy-start | bytes 6291460
  105.7 2.0 %copy-start.1 = (bf16[512,1024]{1,0:T(8,128)(2,1)S(1)}, bf16[512,1024]{1,0:T(8,128)(2,1)}, u32[]{:S(2)}) copy-start(bf16[512,1024]{1,0:T(8,128)(2,1)} %get-tuple-element.8) | copy-start | bytes 3145732

commit v3 on v2

--- a/solution.py
+++ b/solution.py
@@ -17,7 +17,7 @@
     part_ref, inner_ref, master_ref, mom_ref, tok_ref,
     out_master, out_mom, out_keys,
     m_v, mom_v, pay, buf_a, buf_b, buf_x, nm_v, nmom_v, fresh, tok_v, keys_v, acc,
-    load_sem, send_sem, ra, rb, rx, rs, rz, rf, rd, out_sem,
+    part_s, part_sem, load_sem, send_sem, ra, rb, rx, rs, rz, rf, rd, out_sem,
 ):
     J = master_ref.shape[0]
     G = master_ref.shape[2] // W
@@ -53,19 +53,24 @@
         return pltpu.make_async_copy(mom_ref.at[:, :, pl.ds(g * W, W)], mom_v.at[pl.ds(g * J, J)], load_sem.at[2, g])
 
     load_tok = pltpu.make_async_copy(tok_ref, tok_v, load_sem.at[3, 0])
-    for g in range(G):
-        for c in load_mi(g):
-            c.start()
-
+    for c in load_mi(0):
+        c.start()
+
+    load_part = pltpu.make_async_copy(part_ref, part_s, part_sem)
+    load_part.start()
     barrier = pltpu.get_barrier_semaphore()
     for d in (dev_a, dev_b, dev_x, dev_s, dev_u, dev_d, dev_c):
         pl.semaphore_signal(barrier, inc=1, device_id=d, device_id_type=MESH)
     pl.semaphore_wait(barrier, 7)
+    for g in range(1, G):
+        for c in load_mi(g):
+            c.start()
     for g in range(G):
         load_mom(g).start()
     load_tok.start()
 
-    mask = jnp.bitwise_xor(part_ref[0, rep], rep)
+    load_part.wait()
+    mask = jnp.bitwise_xor(part_s[0, rep], rep)
     bit1 = lax.rem(lax.div(mask, 2), 2)
     pick_a = lax.rem(lax.rem(mask, 2) + bit1, 2) == 1
     pick_b = bit1 == 1
@@ -291,7 +296,7 @@
             jax.ShapeDtypeStruct((J, R, cols), f32),
             jax.ShapeDtypeStruct((toks, cols), bf16),
         ),
-        in_specs=[pl.BlockSpec(memory_space=pltpu.SMEM)] + [anyspace] * 4,
+        in_specs=[pl.BlockSpec(memory_space=pltpu.HBM)] * 5,
         out_specs=(anyspace,) * 3,
         scratch_shapes=[
             pltpu.VMEM((C, R, W), f32),
@@ -306,6 +311,8 @@
             pltpu.VMEM((toks, depth), bf16),
             pltpu.VMEM((G, toks, W), bf16),
             pltpu.VMEM((toks, W), f32),
+            pltpu.SMEM((1, 8), jnp.int32),
+            dma,
             dma((4, G)),
             dma((9,)),
             dma((C,)),
@@ -318,7 +325,7 @@
             dma((3, G)),
         ],
         compiler_params=pltpu.CompilerParams(
-            collective_id=0, has_side_effects=True, vmem_limit_bytes=60 * 1024 * 1024
+            collective_id=0, has_side_effects=True, vmem_limit_bytes=47104 * 1024
         ),
         cost_estimate=pl.CostEstimate(
             flops=2 * toks * depth * cols, bytes_accessed=18 * 1024 * 1024, transcendentals=0

time: 109 us -> 107 us (0.982)
  Pallas kernels: 102 us -> 100 us
    pallas_call x1, Pallas kernels: 102 us -> 100 us  [local(): pl.pallas_call(kernel, out_shape=(jax.ShapeDtypeStruct((J, R, cols), f32)...]
where the time goes in v3:
time: 107 us
  Pallas kernels  100 us (93%)
  local copies, waits for them, and re-layouts  5.48 us (5%)
    pallas_call x1, Pallas kernels, local(): pl.pallas_call(kernel, out_shape=(jax.ShapeDtypeStruct((J, R, cols), f32)...  100 us
    unnamed x7, local copies, waits for them, and re-layouts  5.48 us

profile of v3, /device:TPU:1, one launch (start us, length us, event | category | flops | bytes accessed | tf_op | source)
XLA Modules:
  0.0 106.5 jit_solution(17097551667869419696)
XLA Ops:
  0.6 0.0 copy-start
  0.6 1.2 %copy-done = bf16[1,512,1024]{2,1,0:T(8,128)(2,1)S(1)} copy-done((bf16[1,512,1024]{2,1,0:T(8,128)(2,1)S(1)}, bf16[1,512,1024]{2,1,0:T(8,128)(2,1)}, u32[]{:S(2)}) %copy-start) | copy-done | bytes 1048600
  1.9 0.0 copy-start.1
  1.9 0.7 copy-done.1
  2.5 100.4 %gossip_keys.1 = (f32[8,64,1024]{2,1,0:T(8,128)S(1)}, f32[8,64,1024]{2,1,0:T(8,128)S(1)}, bf16[512,1024]{1,0:T(8,128)(2,1)S(1)}) custom-call(s32[1,8]{1,0:T(1,128)S(1)} %copy-done.1, bf16[8,64,1024]{2,1,0:T(8,128)(2,1)S(1)} %bitcast.10, f32[8,64,1024]{2,1,0:T(8,128)} %bitcast.12, f32[8,64,1024]{2,1,0:T(8,128)} %bitcast.13, bf16[512,8192]{1,0:T(8,128)(2,1)} %bitcast.11), custom_call_target="tpu_custom_call" | custom-call | flops 8589934592 | bytes 18874368 | tf_op jit(solution)/shard_map/gossip_keys/pallas_call | solution.py:292
  102.9 1.3 %copy.11 = f32[1,512,1024]{2,1,0:T(8,128)} copy(f32[1,512,1024]{2,1,0:T(8,128)S(1)} %bitcast.8) | data formatting | bytes 4194304
  104.3 1.3 %copy.12 = f32[1,512,1024]{2,1,0:T(8,128)} copy(f32[1,512,1024]{2,1,0:T(8,128)S(1)} %bitcast.7) | data formatting | bytes 4194304
  105.6 1.0 copy.13
Async XLA Ops:
  0.6 1.2 %copy-start = (bf16[1,512,1024]{2,1,0:T(8,128)(2,1)S(1)}, bf16[1,512,1024]{2,1,0:T(8,128)(2,1)}, u32[]{:S(2)}) copy-start(bf16[1,512,1024]{2,1,0:T(8,128)(2,1)} %param.5) | copy-start | bytes 3145732
  1.9 0.7 copy-start.1

commit v4 on v3

--- a/solution.py
+++ b/solution.py
@@ -10,14 +10,16 @@
 MESH = pl.DeviceIdType.MESH
 R, W = 64, 256
 SUB = 128
-OFF_B, OFF_X, OFF_U, OFF_Z, OFF_F, OFF_D, OFF_M = 2, 4, 6, 8, 10, 12, 14
+OFF_2, OFF_3, OFF_U, OFF_Z, OFF_F, OFF_D, OFF_M = 3, 5, 7, 9, 11, 13, 15
+LATE = 2
+EARLY = OFF_Z - OFF_U
 
 
 def kernel(
     part_ref, inner_ref, master_ref, mom_ref, tok_ref,
     out_master, out_mom, out_keys,
-    m_v, mom_v, pay, buf_a, buf_b, buf_x, nm_v, nmom_v, fresh, tok_v, keys_v, acc,
-    part_s, part_sem, load_sem, send_sem, ra, rb, rx, rs, rz, rf, rd, out_sem,
+    m_v, mom_v, pay, buf_1, buf_2, buf_3, nm_v, nmom_v, fresh, tok_v, keys_v, acc,
+    part_s, part_sem, load_sem, send_sem, r1, r2, r3, rs, rz, rf, rd, out_sem,
 ):
     J = master_ref.shape[0]
     G = master_ref.shape[2] // W
@@ -39,8 +41,9 @@
     zu = lax.rem(fs + 4, 16)
     zd = lax.rem(fs + 12, 16)
 
-    dev_a, dev_b, dev_x = (rep1, fs), (rep3, fs), (rep4, fs)
+    dev_x, dev_a, dev_b = (rep4, fs), (rep1, fs), (rep3, fs)
     dev_s, dev_u, dev_d, dev_c = (rep, xn), (rep, zu), (rep, zd), (rep, sib)
+    dev_xu, dev_xd = (rep, lax.rem(xn + 4, 16)), (rep, lax.rem(xn + 12, 16))
 
     def load_mi(g):
         cols = pl.ds(g * W, W)
@@ -59,9 +62,9 @@
     load_part = pltpu.make_async_copy(part_ref, part_s, part_sem)
     load_part.start()
     barrier = pltpu.get_barrier_semaphore()
-    for d in (dev_a, dev_b, dev_x, dev_s, dev_u, dev_d, dev_c):
+    for d in (dev_a, dev_b, dev_x, dev_s, dev_u, dev_d, dev_c, dev_xu, dev_xd):
         pl.semaphore_signal(barrier, inc=1, device_id=d, device_id_type=MESH)
-    pl.semaphore_wait(barrier, 7)
+    pl.semaphore_wait(barrier, 9)
     for g in range(1, G):
         for c in load_mi(g):
             c.start()
@@ -81,23 +84,29 @@
             src_ref=src, dst_ref=dst, send_sem=send_sem.at[k], recv_sem=recv, device_id=dev, device_id_type=MESH
         )
 
-    def copy_a(t):
-        return remote(pay.at[t], buf_a.at[t], 0, ra.at[t], dev_a)
-
-    def copy_b(t):
-        return remote(buf_a.at[t], buf_b.at[t], 1, rb.at[t], dev_b)
-
-    def copy_x(t):
-        return remote(buf_b.at[t], buf_x.at[t], 2, rx.at[t], dev_x)
+    def copy_1(t):
+        return remote(pay.at[t], buf_1.at[t], 0, r1.at[t], dev_x)
+
+    def copy_2(t):
+        return remote(buf_1.at[t], buf_2.at[t], 1, r2.at[t], dev_a)
+
+    def copy_3(t):
+        return remote(buf_2.at[t], buf_3.at[t], 2, r3.at[t], dev_b)
 
     def copy_s(t):
         return remote(fresh.at[t, 0], fresh.at[t, 1], 3, rs.at[t], dev_s)
 
     def copy_up_one(t, slot):
-        return remote(fresh.at[t, slot], fresh.at[t, 6 + slot], 4, rz.at[0, t], dev_u)
+        return remote(fresh.at[t, slot], fresh.at[t, 6 + slot], 4 + 7 * slot, rz.at[0, t], dev_u)
 
     def copy_down_one(t, slot):
-        return remote(fresh.at[t, slot], fresh.at[t, 2 + slot], 5, rz.at[1, t], dev_d)
+        return remote(fresh.at[t, slot], fresh.at[t, 2 + slot], 5 + 7 * slot, rz.at[1, t], dev_d)
+
+    def copy_xup(t):
+        return remote(fresh.at[t, 0], fresh.at[t, 7], 9, rz.at[0, t], dev_xu)
+
+    def copy_xdown(t):
+        return remote(fresh.at[t, 0], fresh.at[t, 3], 10, rz.at[1, t], dev_xd)
 
     def copy_up(t):
         return remote(fresh.at[t, pl.ds(0, 2)], fresh.at[t, pl.ds(6, 2)], 4, rz.at[0, t], dev_u)
@@ -126,6 +135,17 @@
         cols = pl.ds(pl.multiple_of(g * W, W), W)
         return pltpu.make_async_copy(keys_v.at[g], out_keys.at[:, cols], out_sem.at[2, g])
 
+    def forward(t):
+        copy_up(t).wait_recv()
+        copy_fup(t).start()
+        copy_down(t).wait_recv()
+        copy_fdown(t).start()
+
+    def to_sibling(t):
+        copy_fup(t).wait_recv()
+        copy_fdown(t).wait_recv()
+        copy_c(t).start()
+
     def tick(t, _):
         for g in range(G):
             @pl.when(t == g * J)
@@ -136,23 +156,23 @@
         @pl.when(t < C)
         def _():
             pay[t, 0] = m_v[t].astype(jnp.bfloat16)
-            copy_a(t).start()
-
-        tb = t - OFF_B
-
-        @pl.when((tb >= 0) & (tb < C))
-        def _():
-            copy_a(tb).wait_recv()
-            buf_a[tb] = jnp.where(pick_a, buf_a[tb], pay[tb])
-            copy_b(tb).start()
-
-        tx = t - OFF_X
-
-        @pl.when((tx >= 0) & (tx < C))
-        def _():
-            copy_b(tx).wait_recv()
-            buf_b[tx] = jnp.where(pick_b, buf_b[tx], buf_a[tx])
-            copy_x(tx).start()
+            copy_1(t).start()
+
+        t2 = t - OFF_2
+
+        @pl.when((t2 >= 0) & (t2 < C))
+        def _():
+            copy_1(t2).wait_recv()
+            buf_1[t2] = jnp.where(pick_x, buf_1[t2], pay[t2])
+            copy_2(t2).start()
+
+        t3 = t - OFF_3
+
+        @pl.when((t3 >= 0) & (t3 < C))
+        def _():
+            copy_2(t3).wait_recv()
+            buf_2[t3] = jnp.where(pick_a, buf_2[t3], buf_1[t3])
+            copy_3(t3).start()
 
         tu = t - OFF_U
 
@@ -163,8 +183,8 @@
 
         @pl.when((tu >= 0) & (tu < C))
         def _():
-            copy_x(tu).wait_recv()
-            their = jnp.where(pick_x, buf_x[tu], buf_b[tu])
+            copy_3(tu).wait_recv()
+            their = jnp.where(pick_b, buf_3[tu], buf_2[tu])
             their_m = their[0].astype(jnp.float32)
             their_i = their[1].astype(jnp.float32)
             own_m = m_v[tu]
@@ -180,6 +200,11 @@
             copy_up_one(tu, 0).start()
             copy_down_one(tu, 0).start()
 
+            @pl.when(tu >= C - LATE)
+            def _():
+                copy_xup(tu).start()
+                copy_xdown(tu).start()
+
         @pl.when((tu >= 0) & (tu < C) & (lax.rem(tu + C, J) == J - 1))
         def _():
             for c in out_copies(lax.div(tu, J)):
@@ -190,25 +215,33 @@
         @pl.when((tz >= 0) & (tz < C))
         def _():
             copy_s(tz).wait_recv()
-            copy_up_one(tz, 1).start()
-            copy_down_one(tz, 1).start()
+
+            @pl.when(tz < C - LATE)
+            def _():
+                copy_up_one(tz, 1).start()
+                copy_down_one(tz, 1).start()
 
         tf = t - OFF_F
-
-        @pl.when((tf >= 0) & (tf < C))
-        def _():
-            copy_up(tf).wait_recv()
-            copy_fup(tf).start()
-            copy_down(tf).wait_recv()
-            copy_fdown(tf).start()
+        tl = tf + EARLY
+
+        @pl.when((tf >= 0) & (tf < C - LATE))
+        def _():
+            forward(tf)
+
+        @pl.when((tl >= C - LATE) & (tl < C))
+        def _():
+            forward(tl)
 
         td = t - OFF_D
-
-        @pl.when((td >= 0) & (td < C))
-        def _():
-            copy_fup(td).wait_recv()
-            copy_fdown(td).wait_recv()
-            copy_c(td).start()
+        te = td + EARLY
+
+        @pl.when((td >= 0) & (td < C - LATE))
+        def _():
+            to_sibling(td)
+
+        @pl.when((te >= C - LATE) & (te < C))
+        def _():
+            to_sibling(te)
 
         tm = t - OFF_M
 
@@ -262,13 +295,18 @@
 
     lax.fori_loop(0, OFF_M + C + Q - 1, tick, 0)
 
+    early, last = pl.ds(0, C - LATE), pl.ds(C - LATE, LATE)
     everything = (
-        (pay, buf_a, 0, ra.at[0], dev_a),
-        (buf_a, buf_b, 1, rb.at[0], dev_b),
-        (buf_b, buf_x, 2, rx.at[0], dev_x),
+        (pay, buf_1, 0, r1.at[0], dev_x),
+        (buf_1, buf_2, 1, r2.at[0], dev_a),
+        (buf_2, buf_3, 2, r3.at[0], dev_b),
         (fresh.at[:, 0], fresh.at[:, 1], 3, rs.at[0], dev_s),
-        (fresh.at[:, pl.ds(0, 2)], fresh.at[:, pl.ds(6, 2)], 4, rz.at[0, 0], dev_u),
-        (fresh.at[:, pl.ds(0, 2)], fresh.at[:, pl.ds(2, 2)], 5, rz.at[1, 0], dev_d),
+        (fresh.at[:, 0], fresh.at[:, 6], 4, rz.at[0, 0], dev_u),
+        (fresh.at[:, 0], fresh.at[:, 2], 5, rz.at[1, 0], dev_d),
+        (fresh.at[early, 1], fresh.at[early, 7], 11, rz.at[0, 0], dev_u),
+        (fresh.at[early, 1], fresh.at[early, 3], 12, rz.at[1, 0], dev_d),
+        (fresh.at[last, 0], fresh.at[last, 7], 9, rz.at[0, 0], dev_xu),
+        (fresh.at[last, 0], fresh.at[last, 3], 10, rz.at[1, 0], dev_xd),
         (fresh.at[:, 6], fresh.at[:, 4], 6, rf.at[0, 0], dev_u),
         (fresh.at[:, 3], fresh.at[:, 5], 7, rf.at[1, 0], dev_d),
         (fresh.at[:, pl.ds(0, 8)], fresh.at[:, pl.ds(8, 8)], 8, rd.at[0], dev_c),
@@ -314,7 +352,7 @@
             pltpu.SMEM((1, 8), jnp.int32),
             dma,
             dma((4, G)),
-            dma((9,)),
+            dma((13,)),
             dma((C,)),
             dma((C,)),
             dma((C,)),

time: 107 us -> 105 us (0.981)
  Pallas kernels: 100 us -> 98.1 us
    pallas_call x1, Pallas kernels: 100 us -> 98.1 us  [local(): pl.pallas_call(kernel, out_shape=(jax.ShapeDtypeStruct((J, R, cols), f32)...]
where the time goes in v4:
time: 105 us; the launch traced here: 104 us
  Pallas kernels  98.1 us (93%)
  local copies, waits for them, and re-layouts  5.48 us (5%)
    pallas_call x1, Pallas kernels, local(): pl.pallas_call(kernel, out_shape=(jax.ShapeDtypeStruct((J, R, cols), f32)...  98.1 us
    unnamed x7, local copies, waits for them, and re-layouts  5.48 us

profile of v4, /device:TPU:1, one launch (start us, length us, event | category | flops | bytes accessed | tf_op | source)
XLA Modules:
  0.0 104.2 jit_solution(18271388301183099723)
XLA Ops:
  0.6 0.0 copy-start
  0.6 1.2 %copy-done = bf16[1,512,1024]{2,1,0:T(8,128)(2,1)S(1)} copy-done((bf16[1,512,1024]{2,1,0:T(8,128)(2,1)S(1)}, bf16[1,512,1024]{2,1,0:T(8,128)(2,1)}, u32[]{:S(2)}) %copy-start) | copy-done | bytes 1048600
  1.9 0.0 copy-start.1
  1.9 0.7 copy-done.1
  2.5 98.1 %gossip_keys.1 = (f32[8,64,1024]{2,1,0:T(8,128)S(1)}, f32[8,64,1024]{2,1,0:T(8,128)S(1)}, bf16[512,1024]{1,0:T(8,128)(2,1)S(1)}) custom-call(s32[1,8]{1,0:T(1,128)S(1)} %copy-done.1, bf16[8,64,1024]{2,1,0:T(8,128)(2,1)S(1)} %bitcast.10, f32[8,64,1024]{2,1,0:T(8,128)} %bitcast.12, f32[8,64,1024]{2,1,0:T(8,128)} %bitcast.13, bf16[512,8192]{1,0:T(8,128)(2,1)} %bitcast.11), custom_call_target="tpu_custom_call" | custom-call | flops 8589934592 | bytes 18874368 | tf_op jit(solution)/shard_map/gossip_keys/pallas_call | solution.py:330
  100.6 1.3 %copy.11 = f32[1,512,1024]{2,1,0:T(8,128)} copy(f32[1,512,1024]{2,1,0:T(8,128)S(1)} %bitcast.8) | data formatting | bytes 4194304
  101.9 1.3 %copy.12 = f32[1,512,1024]{2,1,0:T(8,128)} copy(f32[1,512,1024]{2,1,0:T(8,128)S(1)} %bitcast.7) | data formatting | bytes 4194304
  103.2 1.0 copy.13
Async XLA Ops:
  0.6 1.2 %copy-start = (bf16[1,512,1024]{2,1,0:T(8,128)(2,1)S(1)}, bf16[1,512,1024]{2,1,0:T(8,128)(2,1)}, u32[]{:S(2)}) copy-start(bf16[1,512,1024]{2,1,0:T(8,128)(2,1)} %param.5) | copy-start | bytes 3145732
  1.9 0.7 copy-start.1

commit v5 on v4

--- a/solution.py
+++ b/solution.py
@@ -12,6 +12,7 @@
 SUB = 128
 OFF_2, OFF_3, OFF_U, OFF_Z, OFF_F, OFF_D, OFF_M = 3, 5, 7, 9, 11, 13, 15
 LATE = 2
+SHARES = 3
 EARLY = OFF_Z - OFF_U
 
 
@@ -19,7 +20,7 @@
     part_ref, inner_ref, master_ref, mom_ref, tok_ref,
     out_master, out_mom, out_keys,
     m_v, mom_v, pay, buf_1, buf_2, buf_3, nm_v, nmom_v, fresh, tok_v, keys_v, acc,
-    part_s, part_sem, load_sem, send_sem, r1, r2, r3, rs, rz, rf, rd, out_sem,
+    part_s, part_sem, load_sem, send_sem, r1, r2, r3, rs, rz, rf, rq, rd, out_sem,
 ):
     J = master_ref.shape[0]
     G = master_ref.shape[2] // W
@@ -119,6 +120,22 @@
 
     def copy_fdown(t):
         return remote(fresh.at[t, 3], fresh.at[t, 5], 7, rf.at[1, t], dev_d)
+
+    def shared(t):
+        first = C - LATE - 2 * SHARES + 1
+        return (t >= first) & (t < C - LATE) & (lax.rem(t + 2 * C - first, 2) == 0)
+
+    def copy_half_up(t):
+        here = pl.ds(0, R // 2)
+        return remote(fresh.at[t, 6, here], fresh.at[t, 4, here], 13, rf.at[0, t], dev_u)
+
+    def copy_half_down(t):
+        here = pl.ds(R // 2, R // 2)
+        return remote(fresh.at[t, 2, here], fresh.at[t, 4, here], 14, rf.at[1, t], dev_d)
+
+    def copy_x(t, i):
+        slot = (6, 2, 4)[i]
+        return remote(fresh.at[t, slot], fresh.at[t, slot + 1], 15 + i, rq.at[i, t], dev_s)
 
     def copy_c(t):
         return remote(fresh.at[t, pl.ds(0, 8)], fresh.at[t, pl.ds(8, 8)], 8, rd.at[t], dev_c)
@@ -216,17 +233,32 @@
         def _():
             copy_s(tz).wait_recv()
 
-            @pl.when(tz < C - LATE)
+            @pl.when((tz < C - LATE) & jnp.logical_not(shared(tz)))
             def _():
                 copy_up_one(tz, 1).start()
                 copy_down_one(tz, 1).start()
 
+            @pl.when(shared(tz))
+            def _():
+                copy_up_one(tz, 0).wait_recv()
+                copy_half_up(tz).start()
+                copy_x(tz, 0).start()
+                copy_down_one(tz, 0).wait_recv()
+                copy_half_down(tz).start()
+                copy_x(tz, 1).start()
+
         tf = t - OFF_F
         tl = tf + EARLY
 
-        @pl.when((tf >= 0) & (tf < C - LATE))
+        @pl.when((tf >= 0) & (tf < C - LATE) & jnp.logical_not(shared(tf)))
         def _():
             forward(tf)
+
+        @pl.when(shared(tf))
+        def _():
+            copy_half_up(tf).wait_recv()
+            copy_half_down(tf).wait_recv()
+            copy_x(tf, 2).start()
 
         @pl.when((tl >= C - LATE) & (tl < C))
         def _():
@@ -235,9 +267,15 @@
         td = t - OFF_D
         te = td + EARLY
 
-        @pl.when((td >= 0) & (td < C - LATE))
+        @pl.when((td >= 0) & (td < C - LATE) & jnp.logical_not(shared(td)))
         def _():
             to_sibling(td)
+
+        @pl.when(shared(td))
+        def _():
+            for i in range(3):
+                copy_x(td, i).wait_recv()
+            copy_c(td).start()
 
         @pl.when((te >= C - LATE) & (te < C))
         def _():
@@ -295,7 +333,8 @@
 
     lax.fori_loop(0, OFF_M + C + Q - 1, tick, 0)
 
-    early, last = pl.ds(0, C - LATE), pl.ds(C - LATE, LATE)
+    early, last = pl.ds(0, C - LATE - SHARES), pl.ds(C - LATE, LATE)
+    plain, some, half = pl.ds(0, C - SHARES), pl.ds(0, SHARES), pl.ds(0, R // 2)
     everything = (
         (pay, buf_1, 0, r1.at[0], dev_x),
         (buf_1, buf_2, 1, r2.at[0], dev_a),
@@ -307,8 +346,13 @@
         (fresh.at[early, 1], fresh.at[early, 3], 12, rz.at[1, 0], dev_d),
         (fresh.at[last, 0], fresh.at[last, 7], 9, rz.at[0, 0], dev_xu),
         (fresh.at[last, 0], fresh.at[last, 3], 10, rz.at[1, 0], dev_xd),
-        (fresh.at[:, 6], fresh.at[:, 4], 6, rf.at[0, 0], dev_u),
-        (fresh.at[:, 3], fresh.at[:, 5], 7, rf.at[1, 0], dev_d),
+        (fresh.at[plain, 6], fresh.at[plain, 4], 6, rf.at[0, 0], dev_u),
+        (fresh.at[plain, 3], fresh.at[plain, 5], 7, rf.at[1, 0], dev_d),
+        (fresh.at[some, 6, half], fresh.at[some, 4, half], 13, rf.at[0, 0], dev_u),
+        (fresh.at[some, 2, half], fresh.at[some, 4, half], 14, rf.at[1, 0], dev_d),
+        (fresh.at[some, 6], fresh.at[some, 7], 15, rq.at[0, 0], dev_s),
+        (fresh.at[some, 2], fresh.at[some, 3], 16, rq.at[1, 0], dev_s),
+        (fresh.at[some, 4], fresh.at[some, 5], 17, rq.at[2, 0], dev_s),
         (fresh.at[:, pl.ds(0, 8)], fresh.at[:, pl.ds(8, 8)], 8, rd.at[0], dev_c),
     )
     for src, dst, k, recv, dev in everything:
@@ -352,13 +396,14 @@
             pltpu.SMEM((1, 8), jnp.int32),
             dma,
             dma((4, G)),
-            dma((13,)),
+            dma((18,)),
             dma((C,)),
             dma((C,)),
             dma((C,)),
             dma((C,)),
             dma((2, C)),
             dma((2, C)),
+            dma((3, C)),
             dma((C,)),
             dma((3, G)),
         ],

time: 105 us -> 104 us (level)
  no operation moved by 1% of the time
where the time goes in v5:
time: 104 us
  Pallas kernels  97.8 us (94%)
  local copies, waits for them, and re-layouts  5.48 us (5%)
    pallas_call x1, Pallas kernels, local(): pl.pallas_call(kernel, out_shape=(jax.ShapeDtypeStruct((J, R, cols), f32)...  97.8 us
    unnamed x7, local copies, waits for them, and re-layouts  5.48 us

profile of v5, /device:TPU:1, one launch (start us, length us, event | category | flops | bytes accessed | tf_op | source)
XLA Modules:
  0.0 103.9 jit_solution(13671484422228885509)
XLA Ops:
  0.6 0.0 copy-start
  0.6 1.2 %copy-done = bf16[1,512,1024]{2,1,0:T(8,128)(2,1)S(1)} copy-done((bf16[1,512,1024]{2,1,0:T(8,128)(2,1)S(1)}, bf16[1,512,1024]{2,1,0:T(8,128)(2,1)}, u32[]{:S(2)}) %copy-start) | copy-done | bytes 1048600
  1.9 0.0 copy-start.1
  1.9 0.7 copy-done.1
  2.5 97.8 %gossip_keys.1 = (f32[8,64,1024]{2,1,0:T(8,128)S(1)}, f32[8,64,1024]{2,1,0:T(8,128)S(1)}, bf16[512,1024]{1,0:T(8,128)(2,1)S(1)}) custom-call(s32[1,8]{1,0:T(1,128)S(1)} %copy-done.1, bf16[8,64,1024]{2,1,0:T(8,128)(2,1)S(1)} %bitcast.10, f32[8,64,1024]{2,1,0:T(8,128)} %bitcast.12, f32[8,64,1024]{2,1,0:T(8,128)} %bitcast.13, bf16[512,8192]{1,0:T(8,128)(2,1)} %bitcast.11), custom_call_target="tpu_custom_call" | custom-call | flops 8589934592 | bytes 18874368 | tf_op jit(solution)/shard_map/gossip_keys/pallas_call | solution.py:374
  100.3 1.3 %copy.11 = f32[1,512,1024]{2,1,0:T(8,128)} copy(f32[1,512,1024]{2,1,0:T(8,128)S(1)} %bitcast.8) | data formatting | bytes 4194304
  101.6 1.3 %copy.12 = f32[1,512,1024]{2,1,0:T(8,128)} copy(f32[1,512,1024]{2,1,0:T(8,128)S(1)} %bitcast.7) | data formatting | bytes 4194304
  102.9 1.0 copy.13
Async XLA Ops:
  0.6 1.2 %copy-start = (bf16[1,512,1024]{2,1,0:T(8,128)(2,1)S(1)}, bf16[1,512,1024]{2,1,0:T(8,128)(2,1)}, u32[]{:S(2)}) copy-start(bf16[1,512,1024]{2,1,0:T(8,128)(2,1)} %param.5) | copy-start | bytes 3145732
  1.9 0.7 copy-start.1

commit v6 on v5

--- a/solution.py
+++ b/solution.py
@@ -10,9 +10,9 @@
 MESH = pl.DeviceIdType.MESH
 R, W = 64, 256
 SUB = 128
-OFF_2, OFF_3, OFF_U, OFF_Z, OFF_F, OFF_D, OFF_M = 3, 5, 7, 9, 11, 13, 15
+OFF_2, OFF_3, OFF_U, OFF_Z, OFF_F, OFF_D, OFF_M = 4, 6, 8, 10, 12, 14, 16
 LATE = 2
-SHARES = 3
+SHARES = 4
 EARLY = OFF_Z - OFF_U
 
 
@@ -263,23 +263,6 @@
         @pl.when((tl >= C - LATE) & (tl < C))
         def _():
             forward(tl)
-
-        td = t - OFF_D
-        te = td + EARLY
-
-        @pl.when((td >= 0) & (td < C - LATE) & jnp.logical_not(shared(td)))
-        def _():
-            to_sibling(td)
-
-        @pl.when(shared(td))
-        def _():
-            for i in range(3):
-                copy_x(td, i).wait_recv()
-            copy_c(td).start()
-
-        @pl.when((te >= C - LATE) & (te < C))
-        def _():
-            to_sibling(te)
 
         tm = t - OFF_M
 
@@ -328,6 +311,23 @@
             def _():
                 keys_v[g] = acc[...].astype(jnp.bfloat16)
                 out_key(g).start()
+
+        td = t - OFF_D
+        te = td + EARLY
+
+        @pl.when((td >= 0) & (td < C - LATE) & jnp.logical_not(shared(td)))
+        def _():
+            to_sibling(td)
+
+        @pl.when(shared(td))
+        def _():
+            for i in range(3):
+                copy_x(td, i).wait_recv()
+            copy_c(td).start()
+
+        @pl.when((te >= C - LATE) & (te < C))
+        def _():
+            to_sibling(te)
 
         return 0
 

time: 104 us -> 104 us (level)
  no operation moved by 1% of the time
where the time goes in v6:
time: 104 us
  Pallas kernels  98 us (94%)
  local copies, waits for them, and re-layouts  5.48 us (5%)
    pallas_call x1, Pallas kernels, local(): pl.pallas_call(kernel, out_shape=(jax.ShapeDtypeStruct((J, R, cols), f32)...  98 us
    unnamed x7, local copies, waits for them, and re-layouts  5.48 us

profile of v6, /device:TPU:1, one launch (start us, length us, event | category | flops | bytes accessed | tf_op | source)
XLA Modules:
  0.0 104.2 jit_solution(13484224309140585120)
XLA Ops:
  0.6 0.0 copy-start
  0.6 1.2 %copy-done = bf16[1,512,1024]{2,1,0:T(8,128)(2,1)S(1)} copy-done((bf16[1,512,1024]{2,1,0:T(8,128)(2,1)S(1)}, bf16[1,512,1024]{2,1,0:T(8,128)(2,1)}, u32[]{:S(2)}) %copy-start) | copy-done | bytes 1048600
  1.9 0.0 copy-start.1
  1.9 0.7 copy-done.1
  2.5 98.0 %gossip_keys.1 = (f32[8,64,1024]{2,1,0:T(8,128)S(1)}, f32[8,64,1024]{2,1,0:T(8,128)S(1)}, bf16[512,1024]{1,0:T(8,128)(2,1)S(1)}) custom-call(s32[1,8]{1,0:T(1,128)S(1)} %copy-done.1, bf16[8,64,1024]{2,1,0:T(8,128)(2,1)S(1)} %bitcast.10, f32[8,64,1024]{2,1,0:T(8,128)} %bitcast.12, f32[8,64,1024]{2,1,0:T(8,128)} %bitcast.13, bf16[512,8192]{1,0:T(8,128)(2,1)} %bitcast.11), custom_call_target="tpu_custom_call" | custom-call | flops 8589934592 | bytes 18874368 | tf_op jit(solution)/shard_map/gossip_keys/pallas_call | solution.py:374
  100.6 1.3 %copy.11 = f32[1,512,1024]{2,1,0:T(8,128)} copy(f32[1,512,1024]{2,1,0:T(8,128)S(1)} %bitcast.8) | data formatting | bytes 4194304
  101.9 1.3 %copy.12 = f32[1,512,1024]{2,1,0:T(8,128)} copy(f32[1,512,1024]{2,1,0:T(8,128)S(1)} %bitcast.7) | data formatting | bytes 4194304
  103.2 1.0 copy.13
Async XLA Ops:
  0.6 1.2 %copy-start = (bf16[1,512,1024]{2,1,0:T(8,128)(2,1)S(1)}, bf16[1,512,1024]{2,1,0:T(8,128)(2,1)}, u32[]{:S(2)}) copy-start(bf16[1,512,1024]{2,1,0:T(8,128)(2,1)} %param.5) | copy-start | bytes 3145732
  1.9 0.7 copy-start.1

commit v7 on v6

--- a/solution.py
+++ b/solution.py
@@ -10,9 +10,9 @@
 MESH = pl.DeviceIdType.MESH
 R, W = 64, 256
 SUB = 128
-OFF_2, OFF_3, OFF_U, OFF_Z, OFF_F, OFF_D, OFF_M = 4, 6, 8, 10, 12, 14, 16
+OFF_2, OFF_3, OFF_U, OFF_Z, OFF_F, OFF_D, OFF_M = 3, 5, 7, 9, 11, 13, 15
 LATE = 2
-SHARES = 4
+SHARES = 3
 EARLY = OFF_Z - OFF_U
 
 

time: 104 us -> 104 us (level)
  no operation moved by 1% of the time
where the time goes in v7:
time: 104 us
  Pallas kernels  97.9 us (94%)
  local copies, waits for them, and re-layouts  5.48 us (5%)
    pallas_call x1, Pallas kernels, local(): pl.pallas_call(kernel, out_shape=(jax.ShapeDtypeStruct((J, R, cols), f32)...  97.9 us
    unnamed x7, local copies, waits for them, and re-layouts  5.48 us

profile of v7, /device:TPU:1, one launch (start us, length us, event | category | flops | bytes accessed | tf_op | source)
XLA Modules:
  0.0 104.0 jit_solution(3126960923294784223)
XLA Ops:
  0.6 0.0 copy-start
  0.6 1.2 %copy-done = bf16[1,512,1024]{2,1,0:T(8,128)(2,1)S(1)} copy-done((bf16[1,512,1024]{2,1,0:T(8,128)(2,1)S(1)}, bf16[1,512,1024]{2,1,0:T(8,128)(2,1)}, u32[]{:S(2)}) %copy-start) | copy-done | bytes 1048600
  1.9 0.0 copy-start.1
  1.9 0.7 copy-done.1
  2.5 97.9 %gossip_keys.1 = (f32[8,64,1024]{2,1,0:T(8,128)S(1)}, f32[8,64,1024]{2,1,0:T(8,128)S(1)}, bf16[512,1024]{1,0:T(8,128)(2,1)S(1)}) custom-call(s32[1,8]{1,0:T(1,128)S(1)} %copy-done.1, bf16[8,64,1024]{2,1,0:T(8,128)(2,1)S(1)} %bitcast.10, f32[8,64,1024]{2,1,0:T(8,128)} %bitcast.12, f32[8,64,1024]{2,1,0:T(8,128)} %bitcast.13, bf16[512,8192]{1,0:T(8,128)(2,1)} %bitcast.11), custom_call_target="tpu_custom_call" | custom-call | flops 8589934592 | bytes 18874368 | tf_op jit(solution)/shard_map/gossip_keys/pallas_call | solution.py:374
  100.4 1.3 %copy.11 = f32[1,512,1024]{2,1,0:T(8,128)} copy(f32[1,512,1024]{2,1,0:T(8,128)S(1)} %bitcast.8) | data formatting | bytes 4194304
  101.7 1.3 %copy.12 = f32[1,512,1024]{2,1,0:T(8,128)} copy(f32[1,512,1024]{2,1,0:T(8,128)S(1)} %bitcast.7) | data formatting | bytes 4194304
  103.0 1.0 copy.13
Async XLA Ops:
  0.6 1.2 %copy-start = (bf16[1,512,1024]{2,1,0:T(8,128)(2,1)S(1)}, bf16[1,512,1024]{2,1,0:T(8,128)(2,1)}, u32[]{:S(2)}) copy-start(bf16[1,512,1024]{2,1,0:T(8,128)(2,1)} %param.5) | copy-start | bytes 3145732
  1.9 0.7 copy-start.1
